TPU v7x, 32 devices: a whole 2x2x4 slice. The times are simulated.
32 devices in a mesh: groups: 2 (over x), dp: 8 (over z, y), ctx: 2 (over core).
Axes of the slice: x: 2, y: 2, z: 4, core: 2. Of those that a mesh axis runs over, the one named last changes fastest.
Arguments:
- queries: bfloat16 [16, 768, 2048], P(('groups', 'dp'), 'ctx'), parts along dimension 0, may hold values from -8 to 8
- keys: bfloat16 [16, 768, 512], P(('groups', 'dp'), 'ctx'), parts along dimension 0, may hold values from -8 to 8
- values: bfloat16 [16, 768, 512], P(('groups', 'dp'), 'ctx'), parts along dimension 0, may hold values from -6 to 6
- out_grad: bfloat16 [16, 768, 2048], P(('groups', 'dp'), 'ctx'), parts along dimension 0, may hold values from -6 to 6
- key_weight: bfloat16 [4096, 512], P('ctx'), may hold values from -0.09375 to 0.09375
- value_weight: bfloat16 [4096, 512], P('ctx'), may hold values from -0.09375 to 0.09375
- suffix_embed: bfloat16 [32, 8, 4096], P(('groups', 'dp'), None, 'ctx'), parts along dimension 0, may hold values from -6 to 6
- class_ids: int32 [16], P(('groups', 'dp')), parts along dimension 0, may hold values from 0 to 15
- class_slot: int32 [32], P('groups'), parts along dimension 0, may hold values from 0 to 15, each once
- pad_offset: int32 [16], P(('groups', 'dp')), parts along dimension 0, may hold values from 0 to 384, as said below
- suffix_pos: int32 [16, 8], P(('groups', 'dp')), parts along dimension 0, may hold values from 0 to 767, as said below
Outputs:
- query_grad: bfloat16 [16, 768, 2048], P(('groups', 'dp'), 'ctx'), parts along dimension 0
- key_grad: bfloat16 [16, 768, 512], P(('groups', 'dp'), 'ctx'), parts along dimension 0
- value_grad: bfloat16 [16, 768, 512], P(('groups', 'dp'), 'ctx'), parts along dimension 0
- suffix_grad: float32 [32, 8, 4096], P(('groups', 'dp'), None, 'ctx'), parts along dimension 0
There are 2 independent parts, one for each index of `groups`. A program takes and returns all parts, laid end to end along the dimension named above; an argument that names none is the same for every part. Nothing has to cross between parts.
Inputs may be any that keep to these rules, and one draw needn't show every extreme that they name: `class_slot`: each class gets a distinct slot. `pad_offset`: reached by some prompt. `suffix_pos`: every suffix position of a prompt is at least its pad_offset; the smallest and the largest are reached.
All inputs are finite; a program needn't handle non-finite values.
Results may differ from a plain program's by a relative error of at most 0.039.
Values may be sent and summed in bfloat16 or wider, within the bound.
A program may use at most 128 MiB of HBM per device.

v0:
```python
import functools
import math

import jax
import jax.numpy as jnp
from jax import lax
from jax.experimental import pallas as pl
from jax.experimental.pallas import tpu as pltpu
from jax.sharding import PartitionSpec as P

HEAD_DIM = 128
TILE = 128
PAD = 16
FILL = -1e30
MESH = pl.DeviceIdType.MESH
F32 = jnp.float32
BF16 = jnp.bfloat16


def dot_nn(a, b):
    return lax.dot_general(a, b, (((1,), (0,)), ((), ())), preferred_element_type=F32)


def dot_nt(a, b):
    return lax.dot_general(a, b, (((1,), (1,)), ((), ())), preferred_element_type=F32)


def kernel(
    dims,
    class_ids,
    class_slot,
    pad_offset,
    suffix_pos,
    embed,
    queries,
    out_grad,
    keys,
    values,
    key_weight,
    value_weight,
    dq_out,
    dk_out,
    dv_out,
    sg_out,
    q_s,
    g_s,
    k_s,
    v_s,
    kt_s,
    wk_s,
    wv_s,
    dq_s,
    dk_s,
    dv_s,
    dk_acc,
    dv_acc,
    part,
    part_in,
    fsend,
    table,
    gsend,
    gbuf,
    w_sem,
    loc_sem,
    ex_send,
    ex_recv,
    p_send,
    p_recv,
    f_send,
    f_recv,
    g_send,
    g_recv,
    dq_loc,
    dq_send,
    dq_recv,
    dkv_loc,
    dkv_send,
    dkv_recv,
):
    dp, rows, group, own_heads = dims
    slots, suffix = embed.shape[0], embed.shape[1]
    length = 2 * rows
    width = group * HEAD_DIM
    half_kv = own_heads * HEAD_DIM
    c = lax.axis_index("ctx")
    me = lax.axis_index("dp")
    other = 1 - c
    everyone = dp * 2
    mine = me * 2 + c

    def device(index):
        return {"dp": lax.div(index, 2), "ctx": lax.rem(index, 2)}

    w_copies = [
        pltpu.make_async_copy(key_weight, wk_s, w_sem.at[0]),
        pltpu.make_async_copy(value_weight, wv_s, w_sem.at[1]),
    ]
    for copy in w_copies:
        copy.start()

    barrier = pltpu.get_barrier_semaphore()

    @pl.loop(1, everyone)
    def _(step):
        to = lax.rem(mine + step, everyone)
        pl.semaphore_signal(barrier, inc=1, device_id=device(to), device_id_type=MESH)

    def pieces(j, who):
        head = who * own_heads + j
        wide = pl.ds(pl.multiple_of(head * width, width), width)
        slim = pl.ds(pl.multiple_of(head * HEAD_DIM, HEAD_DIM), HEAD_DIM)
        at = pl.ds(pl.multiple_of(c * rows, 16), rows)
        at_kv = pl.ds(pl.multiple_of(PAD + c * rows, 16), rows)
        return [
            (queries.at[0, :, wide], q_s.at[j, at]),
            (keys.at[0, :, slim], k_s.at[j, at_kv]),
            (out_grad.at[0, :, wide], g_s.at[j, at]),
            (values.at[0, :, slim], v_s.at[j, at_kv]),
        ]

    def local_copies(j):
        return [
            pltpu.make_async_copy(src, dst, loc_sem.at[j, n])
            for n, (src, dst) in enumerate(pieces(j, c))
        ]

    def remote_copies(j):
        return [
            pltpu.make_async_remote_copy(
                src_ref=src,
                dst_ref=dst,
                send_sem=ex_send.at[j, n],
                recv_sem=ex_recv.at[j, n],
                device_id={"ctx": other},
                device_id_type=MESH,
            )
            for n, (src, dst) in enumerate(pieces(j, other))
        ]

    def incoming(j):
        at = pl.ds(pl.multiple_of(other * rows, 16), rows)
        at_kv = pl.ds(pl.multiple_of(PAD + other * rows, 16), rows)
        dsts = [q_s.at[j, at], k_s.at[j, at_kv], g_s.at[j, at], v_s.at[j, at_kv]]
        return [
            pltpu.make_async_remote_copy(
                src_ref=dst,
                dst_ref=dst,
                send_sem=ex_send.at[j, n],
                recv_sem=ex_recv.at[j, n],
                device_id={"ctx": other},
                device_id_type=MESH,
            )
            for n, dst in enumerate(dsts)
        ]

    for j in range(own_heads):
        for copy in local_copies(j):
            copy.start()

    pl.semaphore_wait(barrier, everyone - 1)

    for j in range(own_heads):
        for copy in remote_copies(j):
            copy.start()

    stacked = jnp.concatenate([embed[s].astype(F32) for s in range(slots)], axis=0).astype(BF16)
    for copy in w_copies:
        copy.wait()
    part[0] = dot_nn(stacked, wk_s[...])
    part[1] = dot_nn(stacked, wv_s[...])

    def head_columns(who):
        return pl.ds(pl.multiple_of(who * half_kv, half_kv), half_kv)

    swap = pltpu.make_async_remote_copy(
        src_ref=part.at[:, :, head_columns(other)],
        dst_ref=part_in,
        send_sem=p_send,
        recv_sem=p_recv,
        device_id={"ctx": other},
        device_id_type=MESH,
    )
    swap.start()
    picked = class_slot[class_ids[0]]
    swap.wait()
    block = slots * suffix
    fsend[0:block] = (part[0, :, head_columns(c)] + part_in[0]).astype(BF16)
    fsend[block : 2 * block] = (part[1, :, head_columns(c)] + part_in[1]).astype(BF16)
    fsend[2 * block : 2 * block + 16] = jnp.full((16, half_kv), picked, jnp.int32).astype(F32).astype(BF16)
    table[me] = fsend[...]

    def forward_copy(to, origin):
        return pltpu.make_async_remote_copy(
            src_ref=fsend,
            dst_ref=table.at[origin],
            send_sem=f_send.at[to],
            recv_sem=f_recv.at[origin],
            device_id={"dp": to},
            device_id_type=MESH,
        )

    @pl.loop(1, dp)
    def _(step):
        forward_copy(lax.rem(me + step, dp), me).start()

    @pl.loop(1, dp)
    def _(step):
        source = lax.rem(me + step, dp)
        forward_copy(source, source).wait_recv()

    found = table[lax.div(picked, slots)].astype(F32)
    which = lax.rem(picked, slots)
    zeros = jnp.zeros((PAD - suffix, half_kv), F32)
    sk = found[0:suffix]
    sv = found[block : block + suffix]
    for s in range(1, slots):
        sk = jnp.where(which == s, found[s * suffix : (s + 1) * suffix], sk)
        sv = jnp.where(which == s, found[block + s * suffix : block + (s + 1) * suffix], sv)
    sk = jnp.concatenate([sk, zeros], axis=0).astype(BF16)
    sv = jnp.concatenate([sv, zeros], axis=0).astype(BF16)
    for j in range(own_heads):
        k_s[j, 0:PAD] = sk[:, j * HEAD_DIM : (j + 1) * HEAD_DIM]
        v_s[j, 0:PAD] = sv[:, j * HEAD_DIM : (j + 1) * HEAD_DIM]

    offset = pad_offset[0]
    lanes = group * TILE
    suffix_row = lax.broadcasted_iota(jnp.int32, (PAD, lanes), 0)
    suffix_at = jnp.full((PAD, lanes), length, jnp.int32)
    for t in range(suffix):
        suffix_at = jnp.where(suffix_row == t, suffix_pos[0, t], suffix_at)
    lane_pos = lax.rem(lax.broadcasted_iota(jnp.int32, (PAD, lanes), 1), TILE)
    diag_key = lax.broadcasted_iota(jnp.int32, (TILE, lanes), 0)
    diag_query = lax.rem(lax.broadcasted_iota(jnp.int32, (TILE, lanes), 1), TILE)
    scale = HEAD_DIM ** (-0.5)
    scale_two = scale * math.log2(math.e)
    tiles = length // TILE
    per_half = tiles // 2

    def own_columns(j):
        return pl.ds(pl.multiple_of((c * own_heads + j) * width, width), width)

    def own_slim(j):
        return pl.ds(pl.multiple_of((c * own_heads + j) * HEAD_DIM, HEAD_DIM), HEAD_DIM)

    def dq_local(j, half):
        src = dq_s.at[j, pl.ds(half * rows, rows)]
        return pltpu.make_async_copy(src, dq_out.at[0, :, own_columns(j)], dq_loc.at[j])

    def dq_remote(j, half):
        return pltpu.make_async_remote_copy(
            src_ref=dq_s.at[j, pl.ds(half * rows, rows)],
            dst_ref=dq_out.at[0, :, own_columns(j)],
            send_sem=dq_send.at[j],
            recv_sem=dq_recv.at[j],
            device_id={"ctx": other},
            device_id_type=MESH,
        )

    def dkv_copies(j):
        here = pl.ds(pl.multiple_of(c * rows, 16), rows)
        there = pl.ds(pl.multiple_of(other * rows, 16), rows)
        local, remote = [], []
        for n, (stage, out) in enumerate(((dk_s, dk_out), (dv_s, dv_out))):
            dst = out.at[0, :, own_slim(j)]
            local.append(pltpu.make_async_copy(stage.at[j, here], dst, dkv_loc.at[j, n]))
            remote.append(
                pltpu.make_async_remote_copy(
                    src_ref=stage.at[j, there],
                    dst_ref=dst,
                    send_sem=dkv_send.at[j, n],
                    recv_sem=dkv_recv.at[j, n],
                    device_id={"ctx": other},
                    device_id_type=MESH,
                )
            )
        return local, remote

    def one_head(j, carry):
        for copy in local_copies(j):
            copy.wait()
        for copy in incoming(j):
            copy.wait_recv()
        kt_s[...] = k_s[j].T
        for i in reversed(range(tiles)):
            at = pl.ds(i * TILE, TILE)
            count = PAD + (i + 1) * TILE
            q4 = jnp.concatenate(
                [q_s[j, at, h * HEAD_DIM : (h + 1) * HEAD_DIM] for h in range(group)], axis=0
            )
            g4 = jnp.concatenate(
                [g_s[j, at, h * HEAD_DIM : (h + 1) * HEAD_DIM] for h in range(group)], axis=0
            )
            scores = dot_nt(k_s[j, 0:count], q4) * scale_two
            seen = [jnp.where(suffix_at <= lane_pos + i * TILE, scores[0:PAD], FILL)]
            if i > 0:
                row = lax.broadcasted_iota(jnp.int32, (i * TILE, lanes), 0)
                seen.append(jnp.where(row >= offset, scores[PAD : PAD + i * TILE], FILL))
            visible = (diag_key == diag_query) | (
                (diag_key < diag_query) & (diag_key + i * TILE >= offset)
            )
            seen.append(jnp.where(visible, scores[PAD + i * TILE :], FILL))
            scores = jnp.concatenate(seen, axis=0)
            row_max = jnp.max(scores, axis=0, keepdims=True)
            expo = jnp.exp2(scores - row_max)
            total = jnp.sum(expo, axis=0, keepdims=True)
            prob_grad = dot_nt(v_s[j, 0:count], g4)
            inverse = 1.0 / total
            delta = jnp.sum(expo * prob_grad, axis=0, keepdims=True) * inverse
            probs = expo * inverse
            score_grad = (probs * (prob_grad - delta)).astype(BF16)
            part_dv = dot_nn(probs.astype(BF16), g4)
            part_dk = dot_nn(score_grad, q4)
            if i == tiles - 1:
                dv_acc[...] = part_dv
                dk_acc[...] = part_dk
            else:
                dv_acc[0:count] += part_dv
                dk_acc[0:count] += part_dk
            dqt = dot_nn(kt_s[:, 0:count], score_grad) * scale
            for h in range(group):
                dq_s[j, at, h * HEAD_DIM : (h + 1) * HEAD_DIM] = dqt[
                    :, h * TILE : (h + 1) * TILE
                ].T.astype(BF16)
            if i % per_half == 0:
                half = i // per_half

                @pl.when(c == half)
                def _():
                    dq_local(j, half).start()

                @pl.when(c != half)
                def _():
                    dq_remote(j, half).start()

        dk_s[j] = (dk_acc[PAD:] * scale).astype(BF16)
        dv_s[j] = dv_acc[PAD:].astype(BF16)
        local, remote = dkv_copies(j)
        for copy in local + remote:
            copy.start()
        ends = jnp.concatenate([dk_acc[0:suffix] * scale, dv_acc[0:suffix]], axis=0)
        gsend[:, pl.ds(pl.multiple_of(j * HEAD_DIM, HEAD_DIM), HEAD_DIM)] = ends.astype(BF16)
        return carry

    lax.fori_loop(0, own_heads, one_head, 0)

    gbuf[mine] = gsend[...]

    def grad_copy(to, origin):
        return pltpu.make_async_remote_copy(
            src_ref=gsend,
            dst_ref=gbuf.at[origin],
            send_sem=g_send.at[to],
            recv_sem=g_recv.at[origin],
            device_id=device(to),
            device_id_type=MESH,
        )

    @pl.loop(1, everyone)
    def _(step):
        grad_copy(lax.rem(mine + step, everyone), mine).start()

    @pl.loop(1, everyone)
    def _(step):
        source = lax.rem(mine + step, everyone)
        grad_copy(source, source).wait_recv()

    def add_prompt(b, sums):
        slot_of = table[b, 2 * block : 2 * block + 16].astype(F32)
        result = []
        for s in range(slots):
            match = slot_of == (me * slots + s).astype(F32)
            for half in range(2):
                term = jnp.where(match, gbuf[b * 2 + half].astype(F32), 0.0)
                result.append(sums[s * 2 + half] + term)
        return tuple(result)

    zero = jnp.zeros((2 * suffix, half_kv), F32)
    sums = lax.fori_loop(0, dp, add_prompt, (zero,) * (2 * slots))
    projected = jnp.zeros((slots * suffix, wk_s.shape[0]), F32)
    for n, weight in enumerate((wk_s, wv_s)):
        full = jnp.concatenate(
            [
                jnp.concatenate(
                    [sums[s * 2 + half][n * suffix : (n + 1) * suffix] for half in range(2)], axis=1
                )
                for s in range(slots)
            ],
            axis=0,
        )
        high = full.astype(BF16)
        low = (full - high.astype(F32)).astype(BF16)
        both = dot_nt(jnp.concatenate([high, low], axis=0), weight[...])
        projected = projected + both[0:block] + both[block:]
    for s in range(slots):
        sg_out[s] = projected[s * suffix : (s + 1) * suffix]

    for j in range(own_heads):
        for copy in remote_copies(j):
            copy.wait_send()
        dq_local(j, 0).wait()
        dq_remote(j, 0).wait()
        local, remote = dkv_copies(j)
        for copy in local + remote:
            copy.wait()

    @pl.loop(1, dp)
    def _(step):
        forward_copy(lax.rem(me + step, dp), me).wait_send()

    @pl.loop(1, everyone)
    def _(step):
        grad_copy(lax.rem(mine + step, everyone), mine).wait_send()


def per_device(
    queries,
    keys,
    values,
    out_grad,
    key_weight,
    value_weight,
    suffix_embed,
    class_ids,
    class_slot,
    pad_offset,
    suffix_pos,
):
    dp = lax.axis_size("dp")
    rows = queries.shape[1]
    kv_width = keys.shape[2]
    group = queries.shape[2] // kv_width
    own_heads = kv_width // HEAD_DIM // 2
    slots, suffix, depth = suffix_embed.shape
    block = slots * suffix
    length = 2 * rows
    width = group * HEAD_DIM
    half_kv = own_heads * HEAD_DIM
    dma = pltpu.SemaphoreType.DMA
    smem = pl.BlockSpec(memory_space=pltpu.SMEM)
    vmem = pl.BlockSpec(memory_space=pltpu.VMEM)
    anywhere = pl.BlockSpec(memory_space=pl.ANY)
    like = lambda x, dtype: jax.ShapeDtypeStruct(x.shape, dtype)
    return pl.pallas_call(
        functools.partial(kernel, (dp, rows, group, own_heads)),
        out_shape=(
            like(queries, BF16),
            like(keys, BF16),
            like(values, BF16),
            like(suffix_embed, F32),
        ),
        in_specs=[smem] * 4 + [vmem] + [anywhere] * 6,
        out_specs=(anywhere, anywhere, anywhere, vmem),
        scratch_shapes=[
            pltpu.VMEM((own_heads, length, width), BF16),
            pltpu.VMEM((own_heads, length, width), BF16),
            pltpu.VMEM((own_heads, PAD + length, HEAD_DIM), BF16),
            pltpu.VMEM((own_heads, PAD + length, HEAD_DIM), BF16),
            pltpu.VMEM((HEAD_DIM, PAD + length), BF16),
            pltpu.VMEM((depth, kv_width), BF16),
            pltpu.VMEM((depth, kv_width), BF16),
            pltpu.VMEM((own_heads, length, width), BF16),
            pltpu.VMEM((own_heads, length, HEAD_DIM), BF16),
            pltpu.VMEM((own_heads, length, HEAD_DIM), BF16),
            pltpu.VMEM((PAD + length, HEAD_DIM), F32),
            pltpu.VMEM((PAD + length, HEAD_DIM), F32),
            pltpu.VMEM((2, block, kv_width), F32),
            pltpu.VMEM((2, block, half_kv), F32),
            pltpu.VMEM((2 * block + 16, half_kv), BF16),
            pltpu.VMEM((dp, 2 * block + 16, half_kv), BF16),
            pltpu.VMEM((2 * suffix, half_kv), BF16),
            pltpu.VMEM((dp * 2, 2 * suffix, half_kv), BF16),
            dma((2,)),
            dma((own_heads, 4)),
            dma((own_heads, 4)),
            dma((own_heads, 4)),
            dma,
            dma,
            dma((dp,)),
            dma((dp,)),
            dma((dp * 2,)),
            dma((dp * 2,)),
            dma((own_heads,)),
            dma((own_heads,)),
            dma((own_heads,)),
            dma((own_heads, 2)),
            dma((own_heads, 2)),
            dma((own_heads, 2)),
        ],
        compiler_params=pltpu.CompilerParams(
            collective_id=0, has_side_effects=True, vmem_limit_bytes=48 * 1024 * 1024
        ),
    )(
        class_ids,
        class_slot,
        pad_offset,
        suffix_pos,
        suffix_embed,
        queries,
        out_grad,
        keys,
        values,
        key_weight,
        value_weight,
    )


def solution(mesh):
    return jax.shard_map(
        per_device,
        mesh=mesh,
        in_specs=(
            P(("groups", "dp"), "ctx", None),
            P(("groups", "dp"), "ctx", None),
            P(("groups", "dp"), "ctx", None),
            P(("groups", "dp"), "ctx", None),
            P("ctx", None),
            P("ctx", None),
            P(("groups", "dp"), None, "ctx"),
            P(("groups", "dp")),
            P("groups"),
            P(("groups", "dp")),
            P(("groups", "dp"), None),
        ),
        out_specs=(
            P(("groups", "dp"), "ctx", None),
            P(("groups", "dp"), "ctx", None),
            P(("groups", "dp"), "ctx", None),
            P(("groups", "dp"), None, "ctx"),
        ),
        check_vma=False,
    )
```

profile of v0, /device:TPU:0, one launch (start us, length us, event | category | flops | bytes accessed | tf_op | source)
XLA Modules:
  0.0 46.8 jit_solution(3638793936809632294)
XLA Ops:
  1.9 0.0 copy-start
  1.9 1.4 %copy-done = bf16[1,384,2048]{2,1,0:T(8,128)(2,1)S(1)} copy-done((bf16[1,384,2048]{2,1,0:T(8,128)(2,1)S(1)}, bf16[1,384,2048]{2,1,0:T(8,128)(2,1)}, u32[]{:S(2)}) %copy-start) | copy-done | bytes 1572888
  3.3 0.0 copy-start.1
  3.3 1.0 %copy-done.1 = bf16[1,384,512]{2,1,0:T(8,128)(2,1)S(1)} copy-done((bf16[1,384,512]{2,1,0:T(8,128)(2,1)S(1)}, bf16[1,384,512]{2,1,0:T(8,128)(2,1)}, u32[]{:S(2)}) %copy-start.1) | copy-done | bytes 393240
  4.3 0.0 copy-start.2
  4.3 1.0 %copy-done.2 = bf16[1,384,512]{2,1,0:T(8,128)(2,1)S(1)} copy-done((bf16[1,384,512]{2,1,0:T(8,128)(2,1)S(1)}, bf16[1,384,512]{2,1,0:T(8,128)(2,1)}, u32[]{:S(2)}) %copy-start.2) | copy-done | bytes 393240
  5.3 0.0 copy-start.3
  5.3 0.8 %copy-done.3 = bf16[2,8,2048]{2,1,0:T(8,128)(2,1)S(1)} copy-done((bf16[2,8,2048]{2,1,0:T(8,128)(2,1)S(1)}, bf16[2,8,2048]{2,1,0:T(8,128)(2,1)}, u32[]{:S(2)}) %copy-start.3) | copy-done | bytes 65560
  6.2 0.0 copy-start.4
  6.2 0.7 %copy-done.4 = s32[16]{0:T(128)S(1)} copy-done((s32[16]{0:T(128)S(1)}, s32[16]{0:T(128)}, u32[]{:S(2)}) %copy-start.4) | copy-done | bytes 88
  6.8 0.0 copy-start.5
  6.8 0.7 %copy-done.5 = s32[1,8]{1,0:T(1,128)S(1)} copy-done((s32[1,8]{1,0:T(1,128)S(1)}, s32[1,8]{1,0:T(1,128)}, u32[]{:S(2)}) %copy-start.5) | copy-done | bytes 56
  7.5 36.0 %shard_map.138 = (bf16[1,384,2048]{2,1,0:T(8,128)(2,1)S(1)}, bf16[1,384,512]{2,1,0:T(8,128)(2,1)S(1)}, bf16[1,384,512]{2,1,0:T(8,128)(2,1)S(1)}, f32[2,8,2048]{2,1,0:T(8,128)S(1)}) custom-call(s32[1]{0:T(128)S(6)} %copy.19.class_ids, s32[16]{0:T(128)S(1)} %copy-done.4, s32[1]{0:T(128)S(6)} %copy.20.pad_offset, s32[1,8]{1,0:T(1,128)S(1)} %copy-done.5, ...), custom_call_target="tpu_custom_call" | custom-call | tf_op jit(solution)/shard_map/pallas_call | solution.py:443
  43.5 1.1 %copy.21 = bf16[1,384,2048]{2,1,0:T(8,128)(2,1)} copy(bf16[1,384,2048]{2,1,0:T(8,128)(2,1)S(1)} %get-tuple-element.8) | data formatting | bytes 3145728
  44.7 0.7 %copy.22 = bf16[1,384,512]{2,1,0:T(8,128)(2,1)} copy(bf16[1,384,512]{2,1,0:T(8,128)(2,1)S(1)} %get-tuple-element.9) | data formatting | bytes 786432
  45.4 0.7 %copy.23 = bf16[1,384,512]{2,1,0:T(8,128)(2,1)} copy(bf16[1,384,512]{2,1,0:T(8,128)(2,1)S(1)} %get-tuple-element.10) | data formatting | bytes 786432
  46.2 0.7 %copy.24 = f32[2,8,2048]{2,1,0:T(8,128)} copy(f32[2,8,2048]{2,1,0:T(8,128)S(1)} %get-tuple-element.11) | data formatting | bytes 262144
Async XLA Ops:
  1.9 1.4 %copy-start = (bf16[1,384,2048]{2,1,0:T(8,128)(2,1)S(1)}, bf16[1,384,2048]{2,1,0:T(8,128)(2,1)}, u32[]{:S(2)}) copy-start(bf16[1,384,2048]{2,1,0:T(8,128)(2,1)} %queries.1) | copy-start | bytes 4718596
  3.3 1.0 %copy-start.1 = (bf16[1,384,512]{2,1,0:T(8,128)(2,1)S(1)}, bf16[1,384,512]{2,1,0:T(8,128)(2,1)}, u32[]{:S(2)}) copy-start(bf16[1,384,512]{2,1,0:T(8,128)(2,1)} %keys.1) | copy-start | bytes 1179652
  4.3 1.0 %copy-start.2 = (bf16[1,384,512]{2,1,0:T(8,128)(2,1)S(1)}, bf16[1,384,512]{2,1,0:T(8,128)(2,1)}, u32[]{:S(2)}) copy-start(bf16[1,384,512]{2,1,0:T(8,128)(2,1)} %values.1) | copy-start | bytes 1179652
  5.3 0.8 %copy-start.3 = (bf16[2,8,2048]{2,1,0:T(8,128)(2,1)S(1)}, bf16[2,8,2048]{2,1,0:T(8,128)(2,1)}, u32[]{:S(2)}) copy-start(bf16[2,8,2048]{2,1,0:T(8,128)(2,1)} %embed.1) | copy-start | bytes 196612
  6.2 0.7 %copy-start.4 = (s32[16]{0:T(128)S(1)}, s32[16]{0:T(128)}, u32[]{:S(2)}) copy-start(s32[16]{0:T(128)} %class_slot.1) | copy-start | bytes 196
  6.8 0.7 %copy-start.5 = (s32[1,8]{1,0:T(1,128)S(1)}, s32[1,8]{1,0:T(1,128)}, u32[]{:S(2)}) copy-start(s32[1,8]{1,0:T(1,128)} %suffix_pos.1) | copy-start | bytes 100
where the time goes:
time: 47.1 us; the launch traced here: 46.8 us
  Pallas kernels  36 us (76%)
  local copies, waits for them, and re-layouts  8.83 us (19%)
  between operations  1.95 us (4%)
    pallas_call x1, Pallas kernels, per_device(): pl.pallas_call(functools.partial(kernel, (dp, rows, group, own_heads)), o...  36 us
    unnamed x16, local copies, waits for them, and re-layouts  8.83 us

commit v1 on v0

--- a/solution.py
+++ b/solution.py
@@ -46,10 +46,16 @@
     g_s,
     k_s,
     v_s,
+    ks_s,
+    vs_s,
     kt_s,
+    expo_s,
+    pg_s,
+    stats,
     wk_s,
     wv_s,
     dq_s,
+    dq_b,
     dk_s,
     dv_s,
     dk_acc,
@@ -68,6 +74,8 @@
     p_recv,
     f_send,
     f_recv,
+    gp_send,
+    gp_recv,
     g_send,
     g_recv,
     dq_loc,
@@ -85,12 +93,6 @@
     c = lax.axis_index("ctx")
     me = lax.axis_index("dp")
     other = 1 - c
-    everyone = dp * 2
-    mine = me * 2 + c
-
-    def device(index):
-        return {"dp": lax.div(index, 2), "ctx": lax.rem(index, 2)}
-
     w_copies = [
         pltpu.make_async_copy(key_weight, wk_s, w_sem.at[0]),
         pltpu.make_async_copy(value_weight, wv_s, w_sem.at[1]),
@@ -100,17 +102,19 @@
 
     barrier = pltpu.get_barrier_semaphore()
 
-    @pl.loop(1, everyone)
+    pl.semaphore_signal(barrier, inc=1, device_id={"ctx": other}, device_id_type=MESH)
+
+    @pl.loop(1, dp)
     def _(step):
-        to = lax.rem(mine + step, everyone)
-        pl.semaphore_signal(barrier, inc=1, device_id=device(to), device_id_type=MESH)
+        to = lax.rem(me + step, dp)
+        pl.semaphore_signal(barrier, inc=1, device_id={"dp": to}, device_id_type=MESH)
 
     def pieces(j, who):
         head = who * own_heads + j
         wide = pl.ds(pl.multiple_of(head * width, width), width)
         slim = pl.ds(pl.multiple_of(head * HEAD_DIM, HEAD_DIM), HEAD_DIM)
         at = pl.ds(pl.multiple_of(c * rows, 16), rows)
-        at_kv = pl.ds(pl.multiple_of(PAD + c * rows, 16), rows)
+        at_kv = pl.ds(pl.multiple_of(c * rows, 16), rows)
         return [
             (queries.at[0, :, wide], q_s.at[j, at]),
             (keys.at[0, :, slim], k_s.at[j, at_kv]),
@@ -139,7 +143,7 @@
 
     def incoming(j):
         at = pl.ds(pl.multiple_of(other * rows, 16), rows)
-        at_kv = pl.ds(pl.multiple_of(PAD + other * rows, 16), rows)
+        at_kv = pl.ds(pl.multiple_of(other * rows, 16), rows)
         dsts = [q_s.at[j, at], k_s.at[j, at_kv], g_s.at[j, at], v_s.at[j, at_kv]]
         return [
             pltpu.make_async_remote_copy(
@@ -157,11 +161,10 @@
         for copy in local_copies(j):
             copy.start()
 
-    pl.semaphore_wait(barrier, everyone - 1)
-
-    for j in range(own_heads):
-        for copy in remote_copies(j):
-            copy.start()
+    pl.semaphore_wait(barrier, dp)
+
+    for copy in remote_copies(0):
+        copy.start()
 
     stacked = jnp.concatenate([embed[s].astype(F32) for s in range(slots)], axis=0).astype(BF16)
     for copy in w_copies:
@@ -203,24 +206,10 @@
     def _(step):
         forward_copy(lax.rem(me + step, dp), me).start()
 
-    @pl.loop(1, dp)
-    def _(step):
-        source = lax.rem(me + step, dp)
-        forward_copy(source, source).wait_recv()
-
-    found = table[lax.div(picked, slots)].astype(F32)
-    which = lax.rem(picked, slots)
-    zeros = jnp.zeros((PAD - suffix, half_kv), F32)
-    sk = found[0:suffix]
-    sv = found[block : block + suffix]
-    for s in range(1, slots):
-        sk = jnp.where(which == s, found[s * suffix : (s + 1) * suffix], sk)
-        sv = jnp.where(which == s, found[block + s * suffix : block + (s + 1) * suffix], sv)
-    sk = jnp.concatenate([sk, zeros], axis=0).astype(BF16)
-    sv = jnp.concatenate([sv, zeros], axis=0).astype(BF16)
-    for j in range(own_heads):
-        k_s[j, 0:PAD] = sk[:, j * HEAD_DIM : (j + 1) * HEAD_DIM]
-        v_s[j, 0:PAD] = sv[:, j * HEAD_DIM : (j + 1) * HEAD_DIM]
+    for j in range(1, own_heads):
+        for before, copy in zip(remote_copies(j - 1), remote_copies(j)):
+            before.wait_send()
+            copy.start()
 
     offset = pad_offset[0]
     lanes = group * TILE
@@ -243,12 +232,12 @@
         return pl.ds(pl.multiple_of((c * own_heads + j) * HEAD_DIM, HEAD_DIM), HEAD_DIM)
 
     def dq_local(j, half):
-        src = dq_s.at[j, pl.ds(half * rows, rows)]
+        src = dq_b.at[j, pl.ds(half * rows, rows)]
         return pltpu.make_async_copy(src, dq_out.at[0, :, own_columns(j)], dq_loc.at[j])
 
     def dq_remote(j, half):
         return pltpu.make_async_remote_copy(
-            src_ref=dq_s.at[j, pl.ds(half * rows, rows)],
+            src_ref=dq_b.at[j, pl.ds(half * rows, rows)],
             dst_ref=dq_out.at[0, :, own_columns(j)],
             send_sem=dq_send.at[j],
             recv_sem=dq_recv.at[j],
@@ -275,39 +264,129 @@
             )
         return local, remote
 
-    def one_head(j, carry):
+    def tile_rows(ref, j, i):
+        at = pl.ds(i * TILE, TILE)
+        return jnp.concatenate(
+            [ref[j, at, h * HEAD_DIM : (h + 1) * HEAD_DIM] for h in range(group)], axis=0
+        )
+
+    def first_row(i):
+        return i * (i + 1) // 2 * TILE
+
+    def prompt_head(j, carry):
         for copy in local_copies(j):
             copy.wait()
         for copy in incoming(j):
             copy.wait_recv()
-        kt_s[...] = k_s[j].T
-        for i in reversed(range(tiles)):
-            at = pl.ds(i * TILE, TILE)
-            count = PAD + (i + 1) * TILE
-            q4 = jnp.concatenate(
-                [q_s[j, at, h * HEAD_DIM : (h + 1) * HEAD_DIM] for h in range(group)], axis=0
-            )
-            g4 = jnp.concatenate(
-                [g_s[j, at, h * HEAD_DIM : (h + 1) * HEAD_DIM] for h in range(group)], axis=0
-            )
-            scores = dot_nt(k_s[j, 0:count], q4) * scale_two
-            seen = [jnp.where(suffix_at <= lane_pos + i * TILE, scores[0:PAD], FILL)]
+        for i in range(tiles):
+            count = (i + 1) * TILE
+            scores = dot_nt(k_s[j, 0:count], tile_rows(q_s, j, i)) * scale_two
+            seen = []
             if i > 0:
                 row = lax.broadcasted_iota(jnp.int32, (i * TILE, lanes), 0)
-                seen.append(jnp.where(row >= offset, scores[PAD : PAD + i * TILE], FILL))
+                seen.append(jnp.where(row >= offset, scores[0 : i * TILE], FILL))
             visible = (diag_key == diag_query) | (
                 (diag_key < diag_query) & (diag_key + i * TILE >= offset)
             )
-            seen.append(jnp.where(visible, scores[PAD + i * TILE :], FILL))
+            seen.append(jnp.where(visible, scores[i * TILE :], FILL))
             scores = jnp.concatenate(seen, axis=0)
             row_max = jnp.max(scores, axis=0, keepdims=True)
             expo = jnp.exp2(scores - row_max)
-            total = jnp.sum(expo, axis=0, keepdims=True)
-            prob_grad = dot_nt(v_s[j, 0:count], g4)
+            prob_grad = dot_nt(v_s[j, 0:count], tile_rows(g_s, j, i))
+            stats[j, i, 0:1] = row_max
+            stats[j, i, 1:2] = jnp.sum(expo, axis=0, keepdims=True)
+            stats[j, i, 2:3] = jnp.sum(expo * prob_grad, axis=0, keepdims=True)
+            expo_s[j, first_row(i) : first_row(i) + count] = expo
+            pg_s[j, first_row(i) : first_row(i) + count] = prob_grad
+        return carry
+
+    lax.fori_loop(0, own_heads, prompt_head, 0)
+
+    @pl.loop(1, dp)
+    def _(step):
+        source = lax.rem(me + step, dp)
+        forward_copy(source, source).wait_recv()
+
+    found = table[lax.div(picked, slots)].astype(F32)
+    which = lax.rem(picked, slots)
+    zeros = jnp.zeros((PAD - suffix, half_kv), F32)
+    sk = found[0:suffix]
+    sv = found[block : block + suffix]
+    for s in range(1, slots):
+        sk = jnp.where(which == s, found[s * suffix : (s + 1) * suffix], sk)
+        sv = jnp.where(which == s, found[block + s * suffix : block + (s + 1) * suffix], sv)
+    sk = jnp.concatenate([sk, zeros], axis=0).astype(BF16)
+    sv = jnp.concatenate([sv, zeros], axis=0).astype(BF16)
+    for j in range(own_heads):
+        ks_s[j] = sk[:, j * HEAD_DIM : (j + 1) * HEAD_DIM]
+        vs_s[j] = sv[:, j * HEAD_DIM : (j + 1) * HEAD_DIM]
+
+    def suffix_head(j, carry):
+        dk_end = jnp.zeros((PAD, HEAD_DIM), F32)
+        dv_end = jnp.zeros((PAD, HEAD_DIM), F32)
+        for i in range(tiles):
+            q4 = tile_rows(q_s, j, i)
+            g4 = tile_rows(g_s, j, i)
+            scores = dot_nt(ks_s[j], q4) * scale_two
+            scores = jnp.where(suffix_at <= lane_pos + i * TILE, scores, FILL)
+            prompt_max = stats[j, i, 0:1]
+            row_max = jnp.maximum(prompt_max, jnp.max(scores, axis=0, keepdims=True))
+            rescale = jnp.exp2(prompt_max - row_max)
+            expo = jnp.exp2(scores - row_max)
+            prob_grad = dot_nt(vs_s[j], g4)
+            total = stats[j, i, 1:2] * rescale + jnp.sum(expo, axis=0, keepdims=True)
             inverse = 1.0 / total
-            delta = jnp.sum(expo * prob_grad, axis=0, keepdims=True) * inverse
+            delta = inverse * (
+                stats[j, i, 2:3] * rescale + jnp.sum(expo * prob_grad, axis=0, keepdims=True)
+            )
+            stats[j, i, 3:4] = rescale * inverse
+            stats[j, i, 4:5] = delta
             probs = expo * inverse
             score_grad = (probs * (prob_grad - delta)).astype(BF16)
+            dv_end = dv_end + dot_nn(probs.astype(BF16), g4)
+            dk_end = dk_end + dot_nn(score_grad, q4)
+            dq_end = lax.dot_general(
+                score_grad, ks_s[j], (((0,), (0,)), ((), ())), preferred_element_type=F32
+            )
+            dq_s[j, pl.ds(i * TILE, TILE)] = jnp.concatenate(
+                [dq_end[h * TILE : (h + 1) * TILE] for h in range(group)], axis=1
+            )
+        ends = jnp.concatenate([dk_end[0:suffix] * scale, dv_end[0:suffix]], axis=0)
+        gsend[c, :, pl.ds(pl.multiple_of(j * HEAD_DIM, HEAD_DIM), HEAD_DIM)] = ends.astype(BF16)
+        return carry
+
+    lax.fori_loop(0, own_heads, suffix_head, 0)
+
+    pair = pltpu.make_async_remote_copy(
+        src_ref=gsend.at[c],
+        dst_ref=gsend.at[c],
+        send_sem=gp_send,
+        recv_sem=gp_recv,
+        device_id={"ctx": other},
+        device_id_type=MESH,
+    )
+    pair.start()
+
+    def grad_copy(to, origin):
+        return pltpu.make_async_remote_copy(
+            src_ref=gsend,
+            dst_ref=gbuf.at[origin],
+            send_sem=g_send.at[to],
+            recv_sem=g_recv.at[origin],
+            device_id={"dp": to},
+            device_id_type=MESH,
+        )
+
+    def prompt_grads(j, carry):
+        kt_s[...] = k_s[j].T
+        for i in reversed(range(tiles)):
+            count = (i + 1) * TILE
+            at = pl.ds(i * TILE, TILE)
+            q4 = tile_rows(q_s, j, i)
+            g4 = tile_rows(g_s, j, i)
+            probs = expo_s[j, first_row(i) : first_row(i) + count] * stats[j, i, 3:4]
+            prob_grad = pg_s[j, first_row(i) : first_row(i) + count]
+            score_grad = (probs * (prob_grad - stats[j, i, 4:5])).astype(BF16)
             part_dv = dot_nn(probs.astype(BF16), g4)
             part_dk = dot_nn(score_grad, q4)
             if i == tiles - 1:
@@ -316,11 +395,11 @@
             else:
                 dv_acc[0:count] += part_dv
                 dk_acc[0:count] += part_dk
-            dqt = dot_nn(kt_s[:, 0:count], score_grad) * scale
+            dqt = dot_nn(kt_s[:, 0:count], score_grad)
             for h in range(group):
-                dq_s[j, at, h * HEAD_DIM : (h + 1) * HEAD_DIM] = dqt[
-                    :, h * TILE : (h + 1) * TILE
-                ].T.astype(BF16)
+                columns = slice(h * HEAD_DIM, (h + 1) * HEAD_DIM)
+                summed = dqt[:, h * TILE : (h + 1) * TILE].T + dq_s[j, at, columns]
+                dq_b[j, at, columns] = (summed * scale).astype(BF16)
             if i % per_half == 0:
                 half = i // per_half
 
@@ -332,36 +411,37 @@
                 def _():
                     dq_remote(j, half).start()
 
-        dk_s[j] = (dk_acc[PAD:] * scale).astype(BF16)
-        dv_s[j] = dv_acc[PAD:].astype(BF16)
+        dk_s[j] = (dk_acc[...] * scale).astype(BF16)
+        dv_s[j] = dv_acc[...].astype(BF16)
         local, remote = dkv_copies(j)
         for copy in local + remote:
             copy.start()
-        ends = jnp.concatenate([dk_acc[0:suffix] * scale, dv_acc[0:suffix]], axis=0)
-        gsend[:, pl.ds(pl.multiple_of(j * HEAD_DIM, HEAD_DIM), HEAD_DIM)] = ends.astype(BF16)
+
+        @pl.when(j == 0)
+        def _():
+            pair.wait_send()
+            gpair_in.wait_recv()
+            gbuf[me] = gsend[...]
+
+            @pl.loop(1, dp)
+            def _(step):
+                grad_copy(lax.rem(me + step, dp), me).start()
+
         return carry
 
-    lax.fori_loop(0, own_heads, one_head, 0)
-
-    gbuf[mine] = gsend[...]
-
-    def grad_copy(to, origin):
-        return pltpu.make_async_remote_copy(
-            src_ref=gsend,
-            dst_ref=gbuf.at[origin],
-            send_sem=g_send.at[to],
-            recv_sem=g_recv.at[origin],
-            device_id=device(to),
-            device_id_type=MESH,
-        )
-
-    @pl.loop(1, everyone)
+    gpair_in = pltpu.make_async_remote_copy(
+        src_ref=gsend.at[other],
+        dst_ref=gsend.at[other],
+        send_sem=gp_send,
+        recv_sem=gp_recv,
+        device_id={"ctx": other},
+        device_id_type=MESH,
+    )
+    lax.fori_loop(0, own_heads, prompt_grads, 0)
+
+    @pl.loop(1, dp)
     def _(step):
-        grad_copy(lax.rem(mine + step, everyone), mine).start()
-
-    @pl.loop(1, everyone)
-    def _(step):
-        source = lax.rem(mine + step, everyone)
+        source = lax.rem(me + step, dp)
         grad_copy(source, source).wait_recv()
 
     def add_prompt(b, sums):
@@ -370,7 +450,7 @@
         for s in range(slots):
             match = slot_of == (me * slots + s).astype(F32)
             for half in range(2):
-                term = jnp.where(match, gbuf[b * 2 + half].astype(F32), 0.0)
+                term = jnp.where(match, gbuf[b, half].astype(F32), 0.0)
                 result.append(sums[s * 2 + half] + term)
         return tuple(result)
 
@@ -395,8 +475,9 @@
         sg_out[s] = projected[s * suffix : (s + 1) * suffix]
 
     for j in range(own_heads):
-        for copy in remote_copies(j):
-            copy.wait_send()
+        if j == own_heads - 1:
+            for copy in remote_copies(j):
+                copy.wait_send()
         dq_local(j, 0).wait()
         dq_remote(j, 0).wait()
         local, remote = dkv_copies(j)
@@ -407,9 +488,21 @@
     def _(step):
         forward_copy(lax.rem(me + step, dp), me).wait_send()
 
-    @pl.loop(1, everyone)
+    @pl.loop(1, dp)
     def _(step):
-        grad_copy(lax.rem(mine + step, everyone), mine).wait_send()
+        grad_copy(lax.rem(me + step, dp), me).wait_send()
+
+
+def write_out(*refs):
+    count = len(refs) // 2
+    sems = refs[-1]
+    copies = [
+        pltpu.make_async_copy(refs[n], refs[count + n], sems.at[n]) for n in range(count)
+    ]
+    for copy in copies:
+        copy.start()
+    for copy in copies:
+        copy.wait()
 
 
 def per_device(
@@ -435,12 +528,14 @@
     length = 2 * rows
     width = group * HEAD_DIM
     half_kv = own_heads * HEAD_DIM
+    tiles = length // TILE
+    pairs = tiles * (tiles + 1) // 2 * TILE
     dma = pltpu.SemaphoreType.DMA
     smem = pl.BlockSpec(memory_space=pltpu.SMEM)
     vmem = pl.BlockSpec(memory_space=pltpu.VMEM)
     anywhere = pl.BlockSpec(memory_space=pl.ANY)
     like = lambda x, dtype: jax.ShapeDtypeStruct(x.shape, dtype)
-    return pl.pallas_call(
+    results = pl.pallas_call(
         functools.partial(kernel, (dp, rows, group, own_heads)),
         out_shape=(
             like(queries, BF16),
@@ -453,22 +548,28 @@
         scratch_shapes=[
             pltpu.VMEM((own_heads, length, width), BF16),
             pltpu.VMEM((own_heads, length, width), BF16),
-            pltpu.VMEM((own_heads, PAD + length, HEAD_DIM), BF16),
-            pltpu.VMEM((own_heads, PAD + length, HEAD_DIM), BF16),
-            pltpu.VMEM((HEAD_DIM, PAD + length), BF16),
+            pltpu.VMEM((own_heads, length, HEAD_DIM), BF16),
+            pltpu.VMEM((own_heads, length, HEAD_DIM), BF16),
+            pltpu.VMEM((own_heads, PAD, HEAD_DIM), BF16),
+            pltpu.VMEM((own_heads, PAD, HEAD_DIM), BF16),
+            pltpu.VMEM((HEAD_DIM, length), BF16),
+            pltpu.VMEM((own_heads, pairs, width), F32),
+            pltpu.VMEM((own_heads, pairs, width), F32),
+            pltpu.VMEM((own_heads, tiles, 8, width), F32),
             pltpu.VMEM((depth, kv_width), BF16),
             pltpu.VMEM((depth, kv_width), BF16),
+            pltpu.VMEM((own_heads, length, width), F32),
             pltpu.VMEM((own_heads, length, width), BF16),
             pltpu.VMEM((own_heads, length, HEAD_DIM), BF16),
             pltpu.VMEM((own_heads, length, HEAD_DIM), BF16),
-            pltpu.VMEM((PAD + length, HEAD_DIM), F32),
-            pltpu.VMEM((PAD + length, HEAD_DIM), F32),
+            pltpu.VMEM((length, HEAD_DIM), F32),
+            pltpu.VMEM((length, HEAD_DIM), F32),
             pltpu.VMEM((2, block, kv_width), F32),
             pltpu.VMEM((2, block, half_kv), F32),
             pltpu.VMEM((2 * block + 16, half_kv), BF16),
             pltpu.VMEM((dp, 2 * block + 16, half_kv), BF16),
-            pltpu.VMEM((2 * suffix, half_kv), BF16),
-            pltpu.VMEM((dp * 2, 2 * suffix, half_kv), BF16),
+            pltpu.VMEM((2, 2 * suffix, half_kv), BF16),
+            pltpu.VMEM((dp, 2, 2 * suffix, half_kv), BF16),
             dma((2,)),
             dma((own_heads, 4)),
             dma((own_heads, 4)),
@@ -477,8 +578,10 @@
             dma,
             dma((dp,)),
             dma((dp,)),
-            dma((dp * 2,)),
-            dma((dp * 2,)),
+            dma,
+            dma,
+            dma((dp,)),
+            dma((dp,)),
             dma((own_heads,)),
             dma((own_heads,)),
             dma((own_heads,)),
@@ -487,7 +590,7 @@
             dma((own_heads, 2)),
         ],
         compiler_params=pltpu.CompilerParams(
-            collective_id=0, has_side_effects=True, vmem_limit_bytes=48 * 1024 * 1024
+            collective_id=0, has_side_effects=True, vmem_limit_bytes=60 * 1024 * 1024
         ),
     )(
         class_ids,
@@ -502,6 +605,13 @@
         key_weight,
         value_weight,
     )
+    return pl.pallas_call(
+        write_out,
+        out_shape=tuple(like(x, x.dtype) for x in results),
+        in_specs=[anywhere] * 4,
+        out_specs=(anywhere,) * 4,
+        scratch_shapes=[dma((4,))],
+    )(*results)
 
 
 def solution(mesh):

time: 47.1 us -> 107 us (2.27)
  Pallas kernels: 36 us -> 105 us
  local copies, waits for them, and re-layouts: 8.83 us -> 0 us
    pallas_call x0 -> x1, Pallas kernels: none -> 76.6 us  [per_device(): pl.pallas_call(write_out, out_shape=tuple((like(x, x.dtype) for x in resu...]
    unnamed x16 -> x0, local copies, waits for them, and re-layouts: 8.83 us -> none
    pallas_call x1, Pallas kernels: 36 us -> 28.8 us  [per_device(): pl.pallas_call(functools.partial(kernel, (dp, rows, group, own_heads)), o...]
where the time goes in v1:
time: 107 us
  Pallas kernels  105 us (98%)
  between operations  1.93 us (2%)
    pallas_call x1, Pallas kernels, per_device(): pl.pallas_call(write_out, out_shape=tuple((like(x, x.dtype) for x in resu...  76.6 us
    pallas_call x1, Pallas kernels, per_device(): pl.pallas_call(functools.partial(kernel, (dp, rows, group, own_heads)), o...  28.8 us

profile of v1, /device:TPU:0, one launch (start us, length us, event | category | flops | bytes accessed | tf_op | source)
XLA Modules:
  0.0 107.3 jit_solution(2153752886453831491)
XLA Ops:
  1.9 28.8 %shard_map.138 = (bf16[1,384,2048]{2,1,0:T(8,128)(2,1)}, bf16[1,384,512]{2,1,0:T(8,128)(2,1)}, bf16[1,384,512]{2,1,0:T(8,128)(2,1)}, f32[2,8,2048]{2,1,0:T(8,128)}) custom-call(s32[1]{0:T(128)S(6)} %copy.15.class_ids, s32[16]{0:T(128)} %class_slot.1, s32[1]{0:T(128)S(6)} %copy.16.pad_offset, s32[1,8]{1,0:T(1,128)} %suffix_pos.1, bf16[2,8,2048]{2,1,0:T(8,128)(2,1)} %embed.1, ...), custom_call_target="tpu_custom_call" | custom-call | tf_op jit(solution)/shard_map/pallas_call | solution.py:538
  30.7 76.6 %shard_map.139 = (bf16[1,384,2048]{2,1,0:T(8,128)(2,1)}, bf16[1,384,512]{2,1,0:T(8,128)(2,1)}, bf16[1,384,512]{2,1,0:T(8,128)(2,1)}, f32[2,8,2048]{2,1,0:T(8,128)}) custom-call(bf16[1,384,2048]{2,1,0:T(8,128)(2,1)} %get-tuple-element.8.refs_0_, bf16[1,384,512]{2,1,0:T(8,128)(2,1)} %get-tuple-element.9.refs_1_, ...), custom_call_target="tpu_custom_call" | custom-call | tf_op jit(solution)/shard_map/pallas_call | solution.py:608

commit v2 on v1

--- a/solution.py
+++ b/solution.py
@@ -31,7 +31,7 @@
     class_slot,
     pad_offset,
     suffix_pos,
-    embed,
+    embed_hbm,
     queries,
     out_grad,
     keys,
@@ -52,6 +52,7 @@
     expo_s,
     pg_s,
     stats,
+    embed,
     wk_s,
     wv_s,
     dq_s,
@@ -94,6 +95,7 @@
     me = lax.axis_index("dp")
     other = 1 - c
     w_copies = [
+        pltpu.make_async_copy(embed_hbm, embed, w_sem.at[2]),
         pltpu.make_async_copy(key_weight, wk_s, w_sem.at[0]),
         pltpu.make_async_copy(value_weight, wv_s, w_sem.at[1]),
     ]
@@ -166,9 +168,9 @@
     for copy in remote_copies(0):
         copy.start()
 
-    stacked = jnp.concatenate([embed[s].astype(F32) for s in range(slots)], axis=0).astype(BF16)
     for copy in w_copies:
         copy.wait()
+    stacked = jnp.concatenate([embed[s].astype(F32) for s in range(slots)], axis=0).astype(BF16)
     part[0] = dot_nn(stacked, wk_s[...])
     part[1] = dot_nn(stacked, wv_s[...])
 
@@ -494,14 +496,24 @@
 
 
 def write_out(*refs):
-    count = len(refs) // 2
-    sems = refs[-1]
-    copies = [
-        pltpu.make_async_copy(refs[n], refs[count + n], sems.at[n]) for n in range(count)
-    ]
-    for copy in copies:
+    count = (len(refs) - 2) // 3
+    sources, results, stages = refs[:count], refs[count : 2 * count], refs[2 * count : 3 * count]
+    read_sem, write_sem = refs[-2:]
+    reads, writes = [], []
+    for n in range(count):
+        rows = sources[n].shape[1]
+        step = TILE if rows % TILE == 0 else rows
+        for at in range(rows // step):
+            part = pl.ds(at * step, step)
+            stage = stages[n].at[:, part]
+            reads.append(pltpu.make_async_copy(sources[n].at[:, part], stage, read_sem.at[n, at]))
+            writes.append(pltpu.make_async_copy(stage, results[n].at[:, part], write_sem.at[n, at]))
+    for copy in reads:
         copy.start()
-    for copy in copies:
+    for before, copy in zip(reads, writes):
+        before.wait()
+        copy.start()
+    for copy in writes:
         copy.wait()
 
 
@@ -543,7 +555,7 @@
             like(values, BF16),
             like(suffix_embed, F32),
         ),
-        in_specs=[smem] * 4 + [vmem] + [anywhere] * 6,
+        in_specs=[smem] * 4 + [anywhere] * 7,
         out_specs=(anywhere, anywhere, anywhere, vmem),
         scratch_shapes=[
             pltpu.VMEM((own_heads, length, width), BF16),
@@ -556,6 +568,7 @@
             pltpu.VMEM((own_heads, pairs, width), F32),
             pltpu.VMEM((own_heads, pairs, width), F32),
             pltpu.VMEM((own_heads, tiles, 8, width), F32),
+            pltpu.VMEM((slots, suffix, depth), BF16),
             pltpu.VMEM((depth, kv_width), BF16),
             pltpu.VMEM((depth, kv_width), BF16),
             pltpu.VMEM((own_heads, length, width), F32),
@@ -570,7 +583,7 @@
             pltpu.VMEM((dp, 2 * block + 16, half_kv), BF16),
             pltpu.VMEM((2, 2 * suffix, half_kv), BF16),
             pltpu.VMEM((dp, 2, 2 * suffix, half_kv), BF16),
-            dma((2,)),
+            dma((3,)),
             dma((own_heads, 4)),
             dma((own_heads, 4)),
             dma((own_heads, 4)),
@@ -605,12 +618,13 @@
         key_weight,
         value_weight,
     )
+    chunks = max(1, rows // TILE)
     return pl.pallas_call(
         write_out,
         out_shape=tuple(like(x, x.dtype) for x in results),
         in_specs=[anywhere] * 4,
         out_specs=(anywhere,) * 4,
-        scratch_shapes=[dma((4,))],
+        scratch_shapes=[pltpu.VMEM(x.shape, x.dtype) for x in results] + [dma((4, chunks)), dma((4, chunks))],
     )(*results)
 
 

time: 107 us -> 33.4 us (0.31)
  Pallas kernels: 105 us -> 31.3 us
    pallas_call x1, Pallas kernels: 76.6 us -> 2.68 us  [per_device(): pl.pallas_call(write_out, out_shape=tuple((like(x, x.dtype) for x in resu...]
where the time goes in v2:
time: 33.4 us; the launch traced here: 33.2 us
  Pallas kernels  31.3 us (94%)
  between operations  1.93 us (6%)
    pallas_call x1, Pallas kernels, per_device(): pl.pallas_call(functools.partial(kernel, (dp, rows, group, own_heads)), o...  28.6 us
    pallas_call x1, Pallas kernels, per_device(): pl.pallas_call(write_out, out_shape=tuple((like(x, x.dtype) for x in resu...  2.68 us

profile of v2, /device:TPU:0, one launch (start us, length us, event | category | flops | bytes accessed | tf_op | source)
XLA Modules:
  0.0 33.2 jit_solution(391165085095805820)
XLA Ops:
  1.9 28.6 %shard_map.138 = (bf16[1,384,2048]{2,1,0:T(8,128)(2,1)}, bf16[1,384,512]{2,1,0:T(8,128)(2,1)}, bf16[1,384,512]{2,1,0:T(8,128)(2,1)}, f32[2,8,2048]{2,1,0:T(8,128)}) custom-call(s32[1]{0:T(128)S(6)} %copy.15.class_ids, s32[16]{0:T(128)} %class_slot.1, s32[1]{0:T(128)S(6)} %copy.16.pad_offset, s32[1,8]{1,0:T(1,128)} %suffix_pos.1, ...), custom_call_target="tpu_custom_call" | custom-call | tf_op jit(solution)/shard_map/pallas_call | solution.py:550
  30.5 2.7 %shard_map.139 = (bf16[1,384,2048]{2,1,0:T(8,128)(2,1)}, bf16[1,384,512]{2,1,0:T(8,128)(2,1)}, bf16[1,384,512]{2,1,0:T(8,128)(2,1)}, f32[2,8,2048]{2,1,0:T(8,128)}) custom-call(bf16[1,384,2048]{2,1,0:T(8,128)(2,1)} %get-tuple-element.8.refs_0_, bf16[1,384,512]{2,1,0:T(8,128)(2,1)} %get-tuple-element.9.refs_1_, ...), custom_call_target="tpu_custom_call" | custom-call | tf_op jit(solution)/shard_map/pallas_call | solution.py:622
